TPU v7x, 32 devices: a whole 2x2x4 slice. The times are simulated.
32 devices in a mesh: parts: 2 (over y), nodes: 4 (over z), feat: 2 (over x), sub: 2 (over core).
Axes of the slice: x: 2, y: 2, z: 4, core: 2. Of those that a mesh axis runs over, the one named last changes fastest.
Arguments:
- features: bfloat16 [16384, 512], P(('parts', 'nodes'), 'feat'), parts along dimension 0, may hold values from -6 to 6
- fetch_tiles: int32 [8, 4, 16], P(('parts', 'nodes'), None, 'sub'), parts along dimension 0, may hold values from 0 to 15
- edge_weights: bfloat16 [8, 4, 16, 128, 128], P(('parts', 'nodes'), None, 'sub'), parts along dimension 0, may hold values from 0 to 4, as said below
- target_slots: int32 [8, 4, 16], P(('parts', 'nodes'), None, 'sub'), parts along dimension 0, may hold values from 0 to 23
- hub_tiles: int32 [8, 4, 4], P(('parts', 'nodes'), None, 'sub'), parts along dimension 0, may hold values from 0 to 15
- degree: int32 [16384], P(('parts', 'nodes')), parts along dimension 0, may hold values from 16 to 63
- w_self: bfloat16 [512, 512], replicated, may hold values from -0.25 to 0.25
- w_neigh: bfloat16 [512, 512], replicated, may hold values from -0.25 to 0.25
- bias: float32 [512], P('feat'), may hold values from -3 to 3
Outputs:
- embedded: bfloat16 [16384, 512], P(('parts', 'nodes', 'sub'), 'feat'), parts along dimension 0
There are 2 independent parts, one for each index of `parts`. A program takes and returns all parts, laid end to end along the dimension named above; an argument that names none is the same for every part. Nothing has to cross between parts.
Inputs may be any that keep to these rules, and one draw needn't show every extreme that they name: `edge_weights`: most entries are zero; a node row receives some tens of nonzero weights in all.
All inputs are finite; a program needn't handle non-finite values.
Results may differ from a plain program's by a relative error of at most 0.003.
Values may be sent and summed in bfloat16 or wider, within the bound.
A program may use at most 64 MiB of HBM per device.

v0:
```python
import jax
import jax.numpy as jnp
from jax import lax
from jax.sharding import PartitionSpec as P


def body(
    features, fetch_tiles, edge_weights, target_slots, hub_tiles, degree, w_self, w_neigh, bias
):
    shards = lax.axis_size("nodes")
    columns = features.shape[1]
    tile = edge_weights.shape[-1]
    tiles_dev = features.shape[0] // tile
    fetch = fetch_tiles.shape[2]
    hub_count = hub_tiles.shape[2]
    half = features.shape[0] // lax.axis_size("sub")
    first_row = lax.axis_index("sub") * half
    first_col = lax.axis_index("feat") * columns
    self_rows = lax.dynamic_slice_in_dim(features, first_row, half, 0)
    self_cols = lax.dynamic_slice_in_dim(w_self, first_col, columns, 1)
    neigh_cols = lax.dynamic_slice_in_dim(w_neigh, first_col, columns, 1)

    def fold_with(weight_cols, carry, piece):
        return carry + jnp.dot(piece, weight_cols, preferred_element_type=jnp.float32)

    empty = jnp.zeros((half, columns), jnp.float32)
    self_proj = fold_with(self_cols, empty, lax.all_gather(self_rows, "feat", axis=1, tiled=True))
    own_tiles = features.reshape(tiles_dev, tile, columns)
    outgoing = own_tiles[fetch_tiles[0]]
    arrived = lax.all_to_all(outgoing, "nodes", split_axis=0, concat_axis=0, tiled=True)
    contrib = jnp.einsum(
        "spij,spjc->spic", edge_weights[0], arrived, preferred_element_type=jnp.float32
    )
    slots_out = tiles_dev + shards * hub_count
    partials = jnp.zeros((slots_out, tile, columns), jnp.float32)
    partials = partials.at[target_slots[0].reshape(-1)].add(
        contrib.reshape(shards * fetch, tile, columns)
    )
    returning = partials[tiles_dev:].reshape(shards, hub_count, tile * columns)
    received = lax.all_to_all(returning, "nodes", split_axis=0, concat_axis=0, tiled=True)
    summed = (
        partials[:tiles_dev]
        .at[hub_tiles[0].reshape(-1)]
        .add(received.reshape(shards * hub_count, tile, columns))
    )
    core_rows = lax.psum_scatter(
        summed.reshape(tiles_dev * tile, columns), "sub", scatter_dimension=0, tiled=True
    )
    divisor = lax.dynamic_slice_in_dim(degree, first_row, half, 0).astype(jnp.float32)
    agg = (core_rows / divisor[:, None]).astype(jnp.bfloat16)
    projected = fold_with(neigh_cols, self_proj, lax.all_gather(agg, "feat", axis=1, tiled=True))
    pre = projected + bias[None, :]
    return jnp.maximum(pre, 0.0).astype(jnp.bfloat16)


def solution(mesh):
    return jax.shard_map(
        body,
        mesh=mesh,
        in_specs=(
            P(("parts", "nodes"), "feat"),
            P(("parts", "nodes"), None, "sub"),
            P(("parts", "nodes"), None, "sub", None, None),
            P(("parts", "nodes"), None, "sub"),
            P(("parts", "nodes"), None, "sub"),
            P(("parts", "nodes")),
            P(),
            P(),
            P("feat"),
        ),
        out_specs=P(("parts", "nodes", "sub"), "feat"),
        check_vma=False,
    )
```

profile of v0, /device:TPU:9, one launch (start us, length us, event | category | flops | bytes accessed | tf_op | source)
XLA Modules:
  0.0 180.9 jit_solution(5445809347291814876)
XLA Ops:
  7.4 0.8 compare_select_fusion
  8.1 0.1 reshape.108
  8.2 0.4 copy-done
  8.6 0.7 gather_fusion
  9.3 2.9 %copy.11 = bf16[32,128,256]{1,2,0:T(8,128)(2,1)} copy(bf16[32,128,256]{2,1,0:T(8,128)(2,1)S(1)} %gather_fusion) | data formatting | bytes 4194304 | tf_op jit(solution)/shard_map/gather | solution.py:29
  12.2 4.9 %all-to-all-start = ((bf16[4,8,128,256]{2,3,1,0:T(8,128)(2,1)}), bf16[4,8,128,256]{2,3,1,0:T(8,128)(2,1)S(1)}, u32[]{:S(2)}, u32[]{:S(2)}) async-start(bf16[4,8,128,256]{2,3,1,0:T(8,128)(2,1)} %bitcast.23), calls=%async_computation | async-start | bytes 4194304 | tf_op jit(solution)/shard_map/all_to_all | solution.py:30
  17.1 0.1 reshape_squeeze.6
  17.2 44.2 %all-to-all-done = bf16[4,8,128,256]{2,3,1,0:T(8,128)(2,1)S(1)} async-done(((bf16[4,8,128,256]{2,3,1,0:T(8,128)(2,1)}), bf16[4,8,128,256]{2,3,1,0:T(8,128)(2,1)S(1)}, u32[]{:S(2)}, u32[]{:S(2)}) %all-to-all-start) | async-done | bytes 2097184 | tf_op jit(solution)/shard_map/all_to_all | solution.py:30
  61.4 3.9 %fusion.3 = f32[4,8,256,128]{3,2,1,0:T(8,128)} fusion(bf16[4,8,128,256]{2,3,1,0:T(8,128)(2,1)S(1)} %all-to-all-done, bf16[1,4,8,128,128]{4,3,2,1,0:T(8,128)(2,1)} %param.11), kind=kOutput, calls=%fused_computation.7 | convolution fusion | flops 268435456 | bytes 7340032 | tf_op jit(solution)/shard_map/spij,spjc->spic/dot_general | solution.py:31
  65.3 5.6 %copy.12 = f32[32,128,256]{2,1,0:T(8,128)} copy(f32[32,128,256]{1,2,0:T(8,128)} %bitcast.21) | data formatting | bytes 8388608 | tf_op jit(solution)/shard_map/reshape | solution.py:37
  70.9 2.0 %broadcast_in_dim.2 = f32[24,128,256]{2,1,0:T(8,128)} broadcast(f32[]{:T(128)} %constant.3.clone.1), dimensions={} | broadcast | bytes 3145732 | tf_op jit(solution)/shard_map/broadcast_in_dim | solution.py:35
  72.9 9.8 %scatter_fusion = f32[24,128,256]{2,1,0:T(8,128)} fusion(f32[24,128,256]{2,1,0:T(8,128)} %broadcast_in_dim.2, s32[32]{0:T(128)S(1)} %fusion.10, f32[32,128,256]{2,1,0:T(8,128)} %copy.12), kind=kCustom, calls=%fused_computation.1 | custom fusion | flops 1048576 | bytes 12583040 | tf_op jit(solution)/shard_map/scatter-add | solution.py:36
  82.7 1.3 slice.11
  84.0 1.7 reshape.103
  85.7 7.8 %all-to-all-start.1 = ((f32[4,2,32768]{2,1,0:T(2,128)}), f32[4,2,32768]{2,1,0:T(2,128)}, u32[]{:S(2)}, u32[]{:S(2)}) async-start(f32[4,2,32768]{2,1,0:T(2,128)} %reshape.103), calls=%async_computation.1 | async-start | bytes 2097152 | tf_op jit(solution)/shard_map/all_to_all | solution.py:40
  93.6 0.1 copy.13
  93.7 0.1 reshape_squeeze.7
  93.7 1.8 slice.10
  95.5 19.6 %all-to-all-done.1 = f32[4,2,32768]{2,1,0:T(2,128)} async-done(((f32[4,2,32768]{2,1,0:T(2,128)}), f32[4,2,32768]{2,1,0:T(2,128)}, u32[]{:S(2)}, u32[]{:S(2)}) %all-to-all-start.1) | async-done | bytes 1048608 | tf_op jit(solution)/shard_map/all_to_all | solution.py:40
  115.1 3.1 %reshape.126 = f32[8,128,256]{2,1,0:T(8,128)} reshape(f32[4,2,32768]{2,1,0:T(2,128)} %all-to-all-done.1) | data formatting | bytes 2097152 | tf_op jit(solution)/shard_map/reshape | solution.py:44
  118.3 2.5 %scatter_fusion.1 = f32[16,128,256]{2,1,0:T(8,128)S(1)} fusion(f32[16,128,256]{2,1,0:T(8,128)S(1)} %slice.10, s32[8]{0:T(128)S(1)} %fusion.11, f32[8,128,256]{2,1,0:T(8,128)} %reshape.126), kind=kCustom, calls=%fused_computation.2 | custom fusion | flops 262144 | bytes 3145760 | tf_op jit(solution)/shard_map/scatter-add | solution.py:44
  120.8 1.3 copy-done.1
  122.1 0.0 all-gather.3.cloned.1.call-start
  122.2 0.8 constant_dynamic-slice_fusion
  123.0 0.0 all-gather.3.cloned.1.call-update
  123.0 0.0 all-gather.5.cloned.1.call-start
  123.1 12.7 %reduce-scatter.2.cloned.1.call-done = f32[1024,256]{1,0:T(8,128)} async-done(((f32[2048,256]{1,0:T(8,128)}), f32[1024,256]{1,0:T(8,128)}) %reduce-scatter.2.cloned.1.call-update) | async-done | bytes 1048592 | tf_op jit(solution)/shard_map/reduce_scatter | solution.py:46
  135.8 2.3 %divide_convert_fusion = bf16[1024,256]{1,0:T(8,128)(2,1)} fusion(f32[1024,256]{1,0:T(8,128)} %reduce-scatter.2.cloned.1.call-done, f32[1024]{0:T(1024)S(1)} %dynamic-slice_convert_fusion), kind=kLoop, calls=%fused_computation.9 | loop fusion | flops 524288 | bytes 1576960 | tf_op jit(solution)/shard_map/convert_element_type | solution.py:50
  138.1 10.3 %all-gather.3.cloned.1.call-done = bf16[1024,512]{1,0:T(8,128)(2,1)} async-done(((bf16[1024,256]{1,0:T(8,128)(2,1)}), bf16[1024,512]{1,0:T(8,128)(2,1)}) %all-gather.3.cloned.1.call-update) | async-done | bytes 1048592 | tf_op jit(solution)/shard_map/all_gather | solution.py:27
  148.4 1.7 fusion.6
  150.1 21.0 %all-gather.5.cloned.1.call-done = bf16[1024,512]{1,0:T(8,128)(2,1)} async-done(((bf16[1024,256]{1,0:T(8,128)(2,1)}), bf16[1024,512]{1,0:T(8,128)(2,1)}) %all-gather.5.cloned.1.call-update) | async-done | bytes 1048592 | tf_op jit(solution)/shard_map/all_gather | solution.py:51
  171.0 2.5 %fusion.2 = bf16[1024,256]{1,0:T(8,128)(2,1)} fusion(f32[1024,256]{1,0:T(8,128)S(1)} %fusion.6, bf16[1024,512]{1,0:T(8,128)(2,1)} %all-gather.5.cloned.1.call-done, f32[256]{0:T(256)S(1)} %copy-done.6, bf16[512,512]{1,0:T(8,128)(2,1)S(1)} %copy-done.3, s32[]{:T(128)S(6)} %select_n.39), kind=kOutput, calls=%fused_computation.6 | convolution fusion | flops 269484032 | bytes 2884612 | tf_op jit(solution)/shard_map/dot_general | solution.py:24
  (21 shorter events, 0.1 us)
Async XLA Ops:
  7.4 1.2 copy-start
  12.2 4.9 %copy-start.4 = (s32[1,4,8]{2,1,0:T(4,128)S(1)}, s32[1,4,8]{2,1,0:T(4,128)}, u32[]{:S(2)}) copy-start(s32[1,4,8]{2,1,0:T(4,128)} %param.12) | copy-start | bytes 388
  12.2 49.2 %all-to-all-start = ((bf16[4,8,128,256]{2,3,1,0:T(8,128)(2,1)}), bf16[4,8,128,256]{2,3,1,0:T(8,128)(2,1)S(1)}, u32[]{:S(2)}, u32[]{:S(2)}) async-start(bf16[4,8,128,256]{2,3,1,0:T(8,128)(2,1)} %bitcast.23), calls=%async_computation | async-start | bytes 4194304 | tf_op jit(solution)/shard_map/all_to_all | solution.py:30
  84.0 9.5 %copy-start.7 = (s32[1,4,2]{1,2,0:T(2,128)S(1)}, s32[1,4,2]{1,2,0:T(2,128)}, u32[]{:S(2)}) copy-start(s32[1,4,2]{1,2,0:T(2,128)} %param.13) | copy-start | bytes 100
  85.7 29.4 %all-to-all-start.1 = ((f32[4,2,32768]{2,1,0:T(2,128)}), f32[4,2,32768]{2,1,0:T(2,128)}, u32[]{:S(2)}, u32[]{:S(2)}) async-start(f32[4,2,32768]{2,1,0:T(2,128)} %reshape.103), calls=%async_computation.1 | async-start | bytes 2097152 | tf_op jit(solution)/shard_map/all_to_all | solution.py:40
  93.6 42.3 %reduce-scatter.2.cloned.1.call-start = ((), (), s32[]{:S(2)}) async-start(), calls=%async_computation.4 | async-start | bytes 3145728 | tf_op jit(solution)/shard_map/reduce_scatter | solution.py:46
  120.7 1.3 copy-start.1
  120.7 2.3 %copy-start.5 = (s32[2048]{0:T(1024)S(1)}, s32[2048]{0:T(1024)}, u32[]{:S(2)}) copy-start(s32[2048]{0:T(1024)} %param.14) | copy-start | bytes 24580
  122.1 26.3 %copy-start.2 = (bf16[512,512]{1,0:T(8,128)(2,1)S(1)}, bf16[512,512]{1,0:T(8,128)(2,1)}, u32[]{:S(2)}) copy-start(bf16[512,512]{1,0:T(8,128)(2,1)} %param.15) | copy-start | bytes 1572868
  122.1 26.3 %all-gather.3.cloned.1.call-start = ((), (), s32[]{:S(2)}) async-start(), calls=%async_computation.3 | async-start | bytes 1572864 | tf_op jit(solution)/shard_map/all_gather | solution.py:27
  123.0 48.0 %all-gather.5.cloned.1.call-start = ((), (), s32[]{:S(2)}) async-start(), calls=%async_computation.5 | async-start | bytes 1572864 | tf_op jit(solution)/shard_map/all_gather | solution.py:51
  123.1 47.9 %copy-start.3 = (bf16[512,512]{1,0:T(8,128)(2,1)S(1)}, bf16[512,512]{1,0:T(8,128)(2,1)}, u32[]{:S(2)}) copy-start(bf16[512,512]{1,0:T(8,128)(2,1)} %param.16) | copy-start | bytes 1572868
  123.1 47.9 %copy-start.6 = (f32[256]{0:T(256)S(1)}, f32[256]{0:T(256)}, u32[]{:S(2)}) copy-start(f32[256]{0:T(256)} %param.17) | copy-start | bytes 3076
Sparse Core Ops, SparseCore 0:
  122.2 13.5 reduce-scatter.1
Sparse Core Ops, SparseCore 1:
  124.1 24.2 all-gather.2
  149.9 21.1 all-gather.4
where the time goes:
time: 183 us; the launch traced here: 181 us
  waiting for transfers between devices  108 us (59%)
  local copies, waits for them, and re-layouts  22.1 us (12%)
  other arithmetic  15.3 us (8%)
  between operations  15 us (8%)
  starting transfers between devices  12.8 us (7%)
  matrix products  8 us (4%)
    all_to_all x1, waiting for transfers between devices, body(): lax.all_to_all(outgoing, 'nodes', split_axis=0, concat_axis=0, tiled=True)  44.2 us
    all_gather x1, waiting for transfers between devices, body(): lax.all_gather(agg, 'feat', axis=1, tiled=True)  21 us
    all_to_all x1, waiting for transfers between devices, body(): lax.all_to_all(returning, 'nodes', split_axis=0, concat_axis=0, tiled=True)  19.6 us
    reduce_scatter x1, waiting for transfers between devices, body(): lax.psum_scatter(summed.reshape(tiles_dev * tile, columns), 'sub', scatte...  12.7 us
    all_gather x1, waiting for transfers between devices, body(): lax.all_gather(self_rows, 'feat', axis=1, tiled=True)  10.3 us
    scatter-add x1, other arithmetic, body(): partials.at[target_slots[0].reshape(-1)]  9.78 us
    all_to_all x1, starting transfers between devices, body(): lax.all_to_all(returning, 'nodes', split_axis=0, concat_axis=0, tiled=True)  7.81 us
    reshape x1, local copies, waits for them, and re-layouts, body(): contrib.reshape(shards * fetch, tile, columns)  5.62 us
  transfers between devices with their start and end apart: 5, of which 5 were waited for; matrix products, arithmetic and copies ran while one was open for 4% of the time, Pallas kernels for 0%

commit v1 on v0

v1 whole, which is shorter than its diff:
```python
import functools

import jax
import jax.numpy as jnp
from jax import lax
from jax.experimental import pallas as pl
from jax.experimental.pallas import tpu as pltpu
from jax.sharding import PartitionSpec as P

MESH = pl.DeviceIdType.MESH
CHUNKS = 4


def place(way, k):
    return 0 if k == 0 else 2 * k - 1 + way


def kernel(
    n, nf, fetch, hubs,
    feats, edges, fetch_out, w_self, w_neigh, degree, bias, idx, out,
    xbuf, wts, fetch_in, fetch_s, own_proj, inv, acc, acc2, hub_out, hub_in, sib_out, sib_in,
    local_sem, xs, xr, fs, fr, zs, zr, ss, sr, hs, hr, bs, br, *ys,
):
    me = lax.axis_index("nodes")
    mf = lax.axis_index("feat")
    u = lax.axis_index("sub")
    tiles, tile, cols = feats.shape
    half = tiles // 2
    per = half // CHUNKS
    zero = (2 * n - 1) * fetch
    zero2 = n * hubs
    last_at = n * fetch
    prev2_at = last_at + tiles + n * hubs
    last2_at = prev2_at + n * hubs

    def rows(core, c):
        return pl.ds(core * half + c * per, per)

    def remote(src, dst, send, recv, **where):
        return pltpu.make_async_remote_copy(
            src_ref=src, dst_ref=dst, send_sem=send, recv_sem=recv,
            device_id=where, device_id_type=MESH,
        )

    def x_copy(d, c):
        return remote(
            feats.at[rows(u, c)], xbuf.at[d, pl.ds(c * per, per)],
            xs.at[d - 1, c], xr.at[d - 1, c], feat=lax.rem(mf + d, nf),
        )

    def f_copy(d):
        to = lax.rem(me + d, n)
        return remote(fetch_out.at[to], fetch_in.at[d], fs.at[d - 1], fr.at[d - 1], nodes=to)

    def z_copy(way, k, c):
        return remote(
            ys[place(way, k)].at[rows(u, c)], ys[place(way, k + 1)].at[rows(u, c)],
            zs.at[way, k, c], zr.at[way, k, c], nodes=me + 1 if way == 0 else me - 1,
        )

    def s_copy(p, c, core):
        return remote(
            ys[p].at[rows(core, c)], ys[p].at[rows(core, c)], ss.at[p, c], sr.at[p, c], sub=1 - u
        )

    def h_copy(d):
        return remote(
            hub_out.at[d], hub_in.at[d], hs.at[d - 1], hr.at[d - 1], nodes=lax.rem(me + d, n)
        )

    def b_copy(t):
        return remote(sib_out.at[t], sib_in.at[t], bs.at[t], br.at[t], sub=1 - u)

    def exists(way, k):
        return me >= k if way == 0 else me + k < n

    own_copy = pltpu.make_async_copy(feats.at[pl.ds(u * half, half)], xbuf.at[0], local_sem.at[0])
    own_copy.start()
    wts_copy = pltpu.make_async_copy(edges, wts, local_sem.at[1])
    wts_copy.start()

    barrier = pltpu.get_barrier_semaphore()
    for d in range(1, nf):
        pl.semaphore_signal(barrier, inc=1, device_id={"feat": lax.rem(mf + d, nf)}, device_id_type=MESH)
    for d in range(1, n):
        pl.semaphore_signal(barrier, inc=1, device_id={"nodes": lax.rem(me + d, n)}, device_id_type=MESH)
    pl.semaphore_signal(barrier, inc=1, device_id={"sub": 1 - u}, device_id_type=MESH)
    pl.semaphore_wait(barrier, nf + n - 1)

    for c in range(CHUNKS):
        for d in range(1, nf):
            x_copy(d, c).start()
    for d in range(1, n):
        f_copy(d).start()
    fetch_in[0] = fetch_out[me]
    acc[zero] = jnp.zeros((tile, cols), jnp.float32)
    acc2[zero2] = jnp.zeros((tile, cols), jnp.float32)

    def project(w, c):
        total = None
        for d in range(nf):
            start = pl.multiple_of(lax.rem(mf + nf - d, nf) * cols, cols)
            piece = xbuf[d, c * per:(c + 1) * per].reshape(per * tile, cols)
            term = jnp.dot(piece, w[pl.ds(start, cols), :], preferred_element_type=jnp.float32)
            total = term if total is None else total + term
        return total

    own_copy.wait()
    for c in range(CHUNKS):
        for d in range(1, nf):
            x_copy(d, c).wait_recv()
        y = project(w_neigh, c)
        ys[0][rows(u, c)] = y.astype(jnp.bfloat16).reshape(per, tile, cols)
        for way in range(2):
            pl.when(exists(1 - way, 1))(lambda: z_copy(way, 0, c).start())
        s_copy(0, c, u).start()

    for d in range(1, n):
        f_copy(d).wait_recv()
    to_smem = pltpu.make_async_copy(fetch_in, fetch_s, local_sem.at[2])
    to_smem.start()
    diagonal = lax.broadcasted_iota(jnp.int32, (tile, tile), 0) == lax.broadcasted_iota(
        jnp.int32, (tile, tile), 1
    )
    for c in range(CHUNKS):
        own_proj[c * per:(c + 1) * per] = (project(w_self, c) + bias[...]).reshape(per, tile, cols)
    for t in range(half):
        row = 1.0 / degree[pl.ds(u * half + t, 1), :].astype(jnp.float32)
        inv[t] = jnp.sum(
            jnp.where(diagonal, jnp.broadcast_to(row, (tile, tile)), 0.0), axis=1, keepdims=True
        )
    wts_copy.wait()
    to_smem.wait()

    def contribute(way, k):
        p = place(way, k)
        shard = me - k if way == 0 else me + k
        d = k if way == 0 else (n - k) % n
        for c in range(CHUNKS):
            s_copy(p, c, 1 - u).wait_recv()
        for j in range(fetch):
            term = jnp.dot(
                wts[shard, j], ys[p][fetch_s[d, 0, j]], preferred_element_type=jnp.float32
            )
            acc[p * fetch + j] = acc[idx[shard * fetch + j]] + term

    def arrive(way, k, c):
        z_copy(way, k - 1, c).wait_recv()
        if k < n - 1:
            pl.when(exists(1 - way, 1))(lambda: z_copy(way, k, c).start())
        s_copy(place(way, k), c, u).start()

    for k in range(1, n):
        for c in range(CHUNKS):
            for way in range(2):
                pl.when(exists(way, k))(functools.partial(arrive, way, k, c))
            if c == 0:
                if k == 1:
                    contribute(0, 0)
                else:
                    for way in range(2):
                        pl.when(exists(way, k - 1))(functools.partial(contribute, way, k - 1))
    for way in range(2):
        pl.when(exists(way, n - 1))(functools.partial(contribute, way, n - 1))

    for d in list(range(1, n)) + [0]:
        to = lax.rem(me + d, n)
        for k in range(hubs):
            part = acc[idx[last_at + tiles + to * hubs + k]].astype(jnp.bfloat16)
            if d:
                hub_out[d, k] = part
            else:
                hub_in[0, k] = part
        if d:
            h_copy(d).start()

    for d in range(n):
        if d:
            h_copy(d).wait_recv()
        helper = lax.rem(me + n - d, n)
        for k in range(hubs):
            acc2[d * hubs + k] = acc2[idx[prev2_at + helper * hubs + k]] + hub_in[d, k].astype(
                jnp.float32
            )

    def total(t):
        return acc[idx[last_at + t]] + acc2[idx[last2_at + t]]

    for t in range(half):
        sib_out[t] = total((1 - u) * half + t).astype(jnp.bfloat16)
        b_copy(t).start()
    for t in range(half):
        mine = total(u * half + t)
        b_copy(t).wait_recv()
        pre = own_proj[t] + (mine + sib_in[t].astype(jnp.float32)) * inv[t]
        out[t] = jnp.maximum(pre, 0.0).astype(jnp.bfloat16)

    for c in range(CHUNKS):
        for d in range(1, nf):
            x_copy(d, c).wait_send()
    for d in range(1, n):
        f_copy(d).wait_send()
        h_copy(d).wait_send()
    for t in range(half):
        b_copy(t).wait_send()

    def sent(way, k, c):
        s_copy(place(way, k), c, u).wait_send()
        if k < n - 1:
            pl.when(exists(1 - way, 1))(lambda: z_copy(way, k, c).wait_send())

    for c in range(CHUNKS):
        s_copy(0, c, u).wait_send()
        for way in range(2):
            pl.when(exists(1 - way, 1))(lambda: z_copy(way, 0, c).wait_send())
            for k in range(1, n):
                pl.when(exists(way, k))(functools.partial(sent, way, k, c))


def chain(target, key, count, empty):
    same = target[:, None] == target[None, :]
    before = key[None, :] < key[:, None]
    prev = jnp.max(jnp.where(same & before, key[None, :], -1), axis=1)
    hit = target[None, :] == jnp.arange(count, dtype=jnp.int32)[:, None]
    last = jnp.max(jnp.where(hit, key[None, :], -1), axis=1)
    return jnp.where(prev < 0, empty, prev), jnp.where(last < 0, empty, last)


def body(
    features, fetch_tiles, edge_weights, target_slots, hub_tiles, degree, w_self, w_neigh, bias
):
    n = lax.axis_size("nodes")
    nf = lax.axis_size("feat")
    me = lax.axis_index("nodes")
    cols = features.shape[1]
    tile = edge_weights.shape[-1]
    tiles = features.shape[0] // tile
    half = tiles // 2
    fetch = fetch_tiles.shape[2]
    hubs = hub_tiles.shape[2]
    first_col = lax.axis_index("feat") * cols
    self_cols = lax.dynamic_slice_in_dim(w_self, first_col, cols, 1)
    neigh_cols = lax.dynamic_slice_in_dim(w_neigh, first_col, cols, 1)

    shard = jnp.arange(n, dtype=jnp.int32)
    away = jnp.abs(shard - me)
    slot = jnp.where(shard < me, 2 * away - 1, 2 * away)
    key = (slot[:, None] * fetch + jnp.arange(fetch, dtype=jnp.int32)[None, :]).reshape(-1)
    prev, last = chain(target_slots.reshape(-1), key, tiles + n * hubs, (2 * n - 1) * fetch)
    key2 = (
        ((me - shard) % n)[:, None] * hubs + jnp.arange(hubs, dtype=jnp.int32)[None, :]
    ).reshape(-1)
    prev2, last2 = chain(hub_tiles.reshape(-1), key2, tiles, n * hubs)
    idx = jnp.concatenate([prev, last, prev2, last2])
    fetch_out = jnp.zeros((n, 8, 128), jnp.int32).at[:, 0, :fetch].set(fetch_tiles[0])

    bf16, f32 = jnp.bfloat16, jnp.float32
    vmem = pl.BlockSpec(memory_space=pltpu.VMEM)
    hbm = pl.BlockSpec(memory_space=pl.ANY)
    dma = pltpu.SemaphoreType.DMA
    result = pl.pallas_call(
        functools.partial(kernel, n, nf, fetch, hubs),
        out_shape=jax.ShapeDtypeStruct((half, tile, cols), bf16),
        in_specs=[hbm, hbm, vmem, vmem, vmem, vmem, vmem, pl.BlockSpec(memory_space=pltpu.SMEM)],
        out_specs=vmem,
        scratch_shapes=[
            pltpu.VMEM((nf, half, tile, cols), bf16),
            pltpu.VMEM((n, fetch, tile, tile), bf16),
            pltpu.VMEM((n, 8, 128), jnp.int32),
            pltpu.SMEM((n, 8, 128), jnp.int32),
            pltpu.VMEM((half, tile, cols), f32),
            pltpu.VMEM((half, tile, 1), f32),
            pltpu.VMEM(((2 * n - 1) * fetch + 1, tile, cols), f32),
            pltpu.VMEM((n * hubs + 1, tile, cols), f32),
            pltpu.VMEM((n, hubs, tile, cols), bf16),
            pltpu.VMEM((n, hubs, tile, cols), bf16),
            pltpu.VMEM((half, tile, cols), bf16),
            pltpu.VMEM((half, tile, cols), bf16),
            dma((3,)),
            dma((nf - 1, CHUNKS)),
            dma((nf - 1, CHUNKS)),
            dma((n - 1,)),
            dma((n - 1,)),
            dma((2, n - 1, CHUNKS)),
            dma((2, n - 1, CHUNKS)),
            dma((2 * n - 1, CHUNKS)),
            dma((2 * n - 1, CHUNKS)),
            dma((n - 1,)),
            dma((n - 1,)),
            dma((half,)),
            dma((half,)),
        ]
        + [pltpu.VMEM((tiles, tile, cols), bf16) for _ in range(2 * n - 1)],
        compiler_params=pltpu.CompilerParams(
            collective_id=0, has_side_effects=True, vmem_limit_bytes=56 * 1024 * 1024
        ),
        name="sage_layer",
    )(
        features.reshape(tiles, tile, cols), edge_weights[0], fetch_out, self_cols, neigh_cols,
        degree.reshape(tiles, tile), bias.reshape(1, cols), idx,
    )
    return result.reshape(half * tile, cols)


def solution(mesh):
    return jax.shard_map(
        body,
        mesh=mesh,
        in_specs=(
            P(("parts", "nodes"), "feat"),
            P(("parts", "nodes"), None, "sub"),
            P(("parts", "nodes"), None, "sub", None, None),
            P(("parts", "nodes"), None, "sub"),
            P(("parts", "nodes"), None, "sub"),
            P(("parts", "nodes")),
            P(),
            P(),
            P("feat"),
        ),
        out_specs=P(("parts", "nodes", "sub"), "feat"),
        check_vma=False,
    )
```

time: 183 us -> 71.8 us (0.39)
  the two profiles are of different devices: /device:TPU:9 before, /device:TPU:25 now
where the time goes in v1:
time: 71.8 us; the launch traced here: 71.5 us
  Pallas kernels  63.9 us (89%)
  local copies, waits for them, and re-layouts  6.2 us (9%)
  other arithmetic  1.31 us (2%)
    pallas_call x1, Pallas kernels, body(): pl.pallas_call(functools.partial(kernel, n, nf, fetch, hubs), out_shape=j...  63.9 us
    unnamed x8, local copies, waits for them, and re-layouts  3.41 us
    dynamic_slice x1, local copies, waits for them, and re-layouts, body(): neigh_cols = lax.dynamic_slice_in_dim(w_neigh, first_col, cols, 1)  1.85 us

profile of v1, /device:TPU:25, one launch (start us, length us, event | category | flops | bytes accessed | tf_op | source)
XLA Modules:
  0.0 71.5 jit_solution(9122747672431024708)
XLA Ops:
  0.0 0.0 copy-start.1
  0.0 0.7 copy-done.1
  0.7 0.1 eq.58
  0.8 0.1 iota_add_fusion
  0.9 0.1 add.80
  0.9 0.1 iota_add_fusion.1
  1.0 0.1 add.75
  1.1 0.1 select_reduce_fusion.1
  1.2 0.2 select_reduce_fusion
  1.4 0.0 copy-start.2
  1.4 0.7 copy-done.2
  2.1 0.1 copy.15
  2.2 0.1 eq.65
  2.3 0.2 select_reduce_fusion.3
  2.5 0.1 select_reduce_fusion.2
  2.6 0.0 copy-start
  2.6 0.6 pad_add_fusion.idx
  3.1 0.1 copy-done
  3.2 0.6 scatter.4.fetch_out
  3.8 1.9 %constant_dynamic-slice_fusion = (bf16[512,256]{1,0:T(8,128)(2,1)}, bf16[512,256]{1,0:T(8,128)(2,1)}) fusion(bf16[512,512]{1,0:T(8,128)(2,1)} %param.18, s32[]{:T(128)S(6)} %select_n.55, bf16[512,512]{1,0:T(8,128)(2,1)} %param.17), kind=kLoop, calls=%fused_computation.20 | loop fusion | bytes 1048580 | tf_op jit(solution)/shard_map/dynamic_slice | solution.py:243
  5.7 63.9 %sage_layer.1 = bf16[8,128,256]{2,1,0:T(8,128)(2,1)} custom-call(bf16[16,128,256]{2,1,0:T(8,128)(2,1)} %bitcast.9, bf16[4,8,128,128]{3,2,1,0:T(8,128)(2,1)} %bitcast.10, s32[4,8,128]{2,1,0:T(8,128)} %scatter.4.fetch_out, bf16[512,256]{1,0:T(8,128)(2,1)} %get-tuple-element.18.w_self, bf16[512,256]{1,0:T(8,128)(2,1)} %get-tuple-element.17.w_neigh, ...), custom_call_target="tpu_custom_call" | custom-call | tf_op jit(solution)/shard_map/sage_layer/pallas_call | solution.py:261
  69.6 1.9 %copy.17 = bf16[1024,256]{1,0:T(8,128)(2,1)} copy(bf16[1024,256]{1,0:T(8,128)(2,1)} %bitcast.8) | data formatting | bytes 1048576
  (5 shorter events, 0.0 us)
Async XLA Ops:
  0.0 0.7 copy-start.1
  1.4 0.7 copy-start.2
  2.6 0.7 copy-start

commit v2 on v1

--- a/solution.py
+++ b/solution.py
@@ -8,7 +8,7 @@
 from jax.sharding import PartitionSpec as P
 
 MESH = pl.DeviceIdType.MESH
-CHUNKS = 4
+CHUNKS = 8
 
 
 def place(way, k):
@@ -17,8 +17,8 @@
 
 def kernel(
     n, nf, fetch, hubs,
-    feats, edges, fetch_out, w_self, w_neigh, degree, bias, idx, out,
-    xbuf, wts, fetch_in, fetch_s, own_proj, inv, acc, acc2, hub_out, hub_in, sib_out, sib_in,
+    feats, edges, fetch_tiles, targets, hub_tiles, w_self_in, w_neigh_in, degree, bias, out,
+    xbuf, wts, w_self, w_neigh, fetch_out, fetch_in, fetch_s, prev, last, prev2, last2, own_proj, inv, acc, acc2, hub_out, hub_in, sib_out, sib_in,
     local_sem, xs, xr, fs, fr, zs, zr, ss, sr, hs, hr, bs, br, *ys,
 ):
     me = lax.axis_index("nodes")
@@ -29,9 +29,6 @@
     per = half // CHUNKS
     zero = (2 * n - 1) * fetch
     zero2 = n * hubs
-    last_at = n * fetch
-    prev2_at = last_at + tiles + n * hubs
-    last2_at = prev2_at + n * hubs
 
     def rows(core, c):
         return pl.ds(core * half + c * per, per)
@@ -76,8 +73,18 @@
 
     own_copy = pltpu.make_async_copy(feats.at[pl.ds(u * half, half)], xbuf.at[0], local_sem.at[0])
     own_copy.start()
+    w_copies = []
+    for i, (whole, part) in enumerate(((w_neigh_in, w_neigh), (w_self_in, w_self))):
+        if whole.shape[1] != cols:
+            whole = whole.at[:, pl.ds(pl.multiple_of(mf * cols, cols), cols)]
+        w_copies.append(pltpu.make_async_copy(whole, part, local_sem.at[3 + i]))
+        w_copies[-1].start()
     wts_copy = pltpu.make_async_copy(edges, wts, local_sem.at[1])
     wts_copy.start()
+
+    fetch_out[...] = jnp.zeros_like(fetch_out)
+    for t in range(n):
+        fetch_out[t, 0:1, 0:fetch] = fetch_tiles[t:t + 1, :]
 
     barrier = pltpu.get_barrier_semaphore()
     for d in range(1, nf):
@@ -95,6 +102,40 @@
     fetch_in[0] = fetch_out[me]
     acc[zero] = jnp.zeros((tile, cols), jnp.float32)
     acc2[zero2] = jnp.zeros((tile, cols), jnp.float32)
+
+    spots = [(0, 0)] + [(way, k) for k in range(1, n) for way in range(2)]
+
+    def link(way, k):
+        p = place(way, k)
+        shard = me - k if way == 0 else me + k
+
+        def edge(j, carry):
+            target = targets[shard, j]
+            slot = p * fetch + j
+            prev[slot] = last[target]
+            for g in range(tiles + n * hubs):
+                last[g] = jnp.where(target == g, slot, last[g])
+            return carry
+
+        lax.fori_loop(0, fetch, edge, 0)
+
+    def link_hubs():
+        for g in range(tiles + n * hubs):
+            last[g] = jnp.int32(zero)
+        for g in range(tiles):
+            last2[g] = jnp.int32(zero2)
+
+        def helper(d, carry):
+            row = lax.rem(me + n - d, n)
+            for k in range(hubs):
+                target = hub_tiles[row, k]
+                slot = d * hubs + k
+                prev2[slot] = last2[target]
+                for g in range(tiles):
+                    last2[g] = jnp.where(target == g, slot, last2[g])
+            return carry
+
+        lax.fori_loop(0, n, helper, 0)
 
     def project(w, c):
         total = None
@@ -106,6 +147,7 @@
         return total
 
     own_copy.wait()
+    w_copies[0].wait()
     for c in range(CHUNKS):
         for d in range(1, nf):
             x_copy(d, c).wait_recv()
@@ -114,6 +156,13 @@
         for way in range(2):
             pl.when(exists(1 - way, 1))(lambda: z_copy(way, 0, c).start())
         s_copy(0, c, u).start()
+        if c == 0:
+            link_hubs()
+        elif c <= len(spots):
+            way, k = spots[c - 1]
+            pl.when(exists(way, k))(functools.partial(link, way, k))
+    for way, k in spots[CHUNKS - 1:]:
+        pl.when(exists(way, k))(functools.partial(link, way, k))
 
     for d in range(1, n):
         f_copy(d).wait_recv()
@@ -122,6 +171,7 @@
     diagonal = lax.broadcasted_iota(jnp.int32, (tile, tile), 0) == lax.broadcasted_iota(
         jnp.int32, (tile, tile), 1
     )
+    w_copies[1].wait()
     for c in range(CHUNKS):
         own_proj[c * per:(c + 1) * per] = (project(w_self, c) + bias[...]).reshape(per, tile, cols)
     for t in range(half):
@@ -142,7 +192,7 @@
             term = jnp.dot(
                 wts[shard, j], ys[p][fetch_s[d, 0, j]], preferred_element_type=jnp.float32
             )
-            acc[p * fetch + j] = acc[idx[shard * fetch + j]] + term
+            acc[p * fetch + j] = acc[prev[p * fetch + j]] + term
 
     def arrive(way, k, c):
         z_copy(way, k - 1, c).wait_recv()
@@ -163,28 +213,44 @@
     for way in range(2):
         pl.when(exists(way, n - 1))(functools.partial(contribute, way, n - 1))
 
-    for d in list(range(1, n)) + [0]:
+    def put_hubs(d):
         to = lax.rem(me + d, n)
         for k in range(hubs):
-            part = acc[idx[last_at + tiles + to * hubs + k]].astype(jnp.bfloat16)
+            part = acc[last[tiles + to * hubs + k]].astype(jnp.bfloat16)
             if d:
                 hub_out[d, k] = part
             else:
                 hub_in[0, k] = part
-        if d:
-            h_copy(d).start()
+
+    def sent(way, k, c):
+        z_copy(way, k, c).wait_send()
+
+    for d in range(n):
+        put_hubs(d)
+    inside = (me > 0) & (me < n - 1)
+    for d in range(1, n):
+        to = lax.rem(me + d, n)
+        pl.when(inside & (to > 0) & (to < n - 1))(lambda: h_copy(d).start())
+    for c in range(CHUNKS):
+        for way in range(2):
+            for k in range(n - 1):
+                pl.when(exists(way, k) & exists(1 - way, 1))(functools.partial(sent, way, k, c))
+    for d in range(1, n):
+        to = lax.rem(me + d, n)
+        pl.when(inside & ((to == 0) | (to == n - 1)))(lambda: h_copy(d).start())
+        pl.when(me == n - 1)(lambda: h_copy(d).start())
+        pl.when(me == 0)(lambda: h_copy(n - d).start())
 
     for d in range(n):
         if d:
             h_copy(d).wait_recv()
-        helper = lax.rem(me + n - d, n)
         for k in range(hubs):
-            acc2[d * hubs + k] = acc2[idx[prev2_at + helper * hubs + k]] + hub_in[d, k].astype(
+            acc2[d * hubs + k] = acc2[prev2[d * hubs + k]] + hub_in[d, k].astype(
                 jnp.float32
             )
 
     def total(t):
-        return acc[idx[last_at + t]] + acc2[idx[last2_at + t]]
+        return acc[last[t]] + acc2[last2[t]]
 
     for t in range(half):
         sib_out[t] = total((1 - u) * half + t).astype(jnp.bfloat16)
@@ -193,7 +259,7 @@
         mine = total(u * half + t)
         b_copy(t).wait_recv()
         pre = own_proj[t] + (mine + sib_in[t].astype(jnp.float32)) * inv[t]
-        out[t] = jnp.maximum(pre, 0.0).astype(jnp.bfloat16)
+        out[t] = pre.astype(jnp.bfloat16)
 
     for c in range(CHUNKS):
         for d in range(1, nf):
@@ -204,26 +270,11 @@
     for t in range(half):
         b_copy(t).wait_send()
 
-    def sent(way, k, c):
-        s_copy(place(way, k), c, u).wait_send()
-        if k < n - 1:
-            pl.when(exists(1 - way, 1))(lambda: z_copy(way, k, c).wait_send())
-
     for c in range(CHUNKS):
         s_copy(0, c, u).wait_send()
         for way in range(2):
-            pl.when(exists(1 - way, 1))(lambda: z_copy(way, 0, c).wait_send())
             for k in range(1, n):
-                pl.when(exists(way, k))(functools.partial(sent, way, k, c))
-
-
-def chain(target, key, count, empty):
-    same = target[:, None] == target[None, :]
-    before = key[None, :] < key[:, None]
-    prev = jnp.max(jnp.where(same & before, key[None, :], -1), axis=1)
-    hit = target[None, :] == jnp.arange(count, dtype=jnp.int32)[:, None]
-    last = jnp.max(jnp.where(hit, key[None, :], -1), axis=1)
-    return jnp.where(prev < 0, empty, prev), jnp.where(last < 0, empty, last)
+                pl.when(exists(way, k))(lambda: s_copy(place(way, k), c, u).wait_send())
 
 
 def body(
@@ -231,43 +282,40 @@
 ):
     n = lax.axis_size("nodes")
     nf = lax.axis_size("feat")
-    me = lax.axis_index("nodes")
     cols = features.shape[1]
     tile = edge_weights.shape[-1]
     tiles = features.shape[0] // tile
     half = tiles // 2
     fetch = fetch_tiles.shape[2]
     hubs = hub_tiles.shape[2]
-    first_col = lax.axis_index("feat") * cols
-    self_cols = lax.dynamic_slice_in_dim(w_self, first_col, cols, 1)
-    neigh_cols = lax.dynamic_slice_in_dim(w_neigh, first_col, cols, 1)
-
-    shard = jnp.arange(n, dtype=jnp.int32)
-    away = jnp.abs(shard - me)
-    slot = jnp.where(shard < me, 2 * away - 1, 2 * away)
-    key = (slot[:, None] * fetch + jnp.arange(fetch, dtype=jnp.int32)[None, :]).reshape(-1)
-    prev, last = chain(target_slots.reshape(-1), key, tiles + n * hubs, (2 * n - 1) * fetch)
-    key2 = (
-        ((me - shard) % n)[:, None] * hubs + jnp.arange(hubs, dtype=jnp.int32)[None, :]
-    ).reshape(-1)
-    prev2, last2 = chain(hub_tiles.reshape(-1), key2, tiles, n * hubs)
-    idx = jnp.concatenate([prev, last, prev2, last2])
-    fetch_out = jnp.zeros((n, 8, 128), jnp.int32).at[:, 0, :fetch].set(fetch_tiles[0])
+    if cols % 128:
+        first_col = lax.axis_index("feat") * cols
+        w_self = lax.dynamic_slice_in_dim(w_self, first_col, cols, 1)
+        w_neigh = lax.dynamic_slice_in_dim(w_neigh, first_col, cols, 1)
+    depth = w_self.shape[0]
 
     bf16, f32 = jnp.bfloat16, jnp.float32
     vmem = pl.BlockSpec(memory_space=pltpu.VMEM)
     hbm = pl.BlockSpec(memory_space=pl.ANY)
+    smem = pl.BlockSpec(memory_space=pltpu.SMEM)
     dma = pltpu.SemaphoreType.DMA
     result = pl.pallas_call(
         functools.partial(kernel, n, nf, fetch, hubs),
         out_shape=jax.ShapeDtypeStruct((half, tile, cols), bf16),
-        in_specs=[hbm, hbm, vmem, vmem, vmem, vmem, vmem, pl.BlockSpec(memory_space=pltpu.SMEM)],
+        in_specs=[hbm, hbm, vmem, smem, smem, hbm, hbm, vmem, vmem],
         out_specs=vmem,
         scratch_shapes=[
             pltpu.VMEM((nf, half, tile, cols), bf16),
             pltpu.VMEM((n, fetch, tile, tile), bf16),
+            pltpu.VMEM((depth, cols), bf16),
+            pltpu.VMEM((depth, cols), bf16),
+            pltpu.VMEM((n, 8, 128), jnp.int32),
             pltpu.VMEM((n, 8, 128), jnp.int32),
             pltpu.SMEM((n, 8, 128), jnp.int32),
+            pltpu.SMEM(((2 * n - 1) * fetch,), jnp.int32),
+            pltpu.SMEM((tiles + n * hubs,), jnp.int32),
+            pltpu.SMEM((n * hubs,), jnp.int32),
+            pltpu.SMEM((tiles,), jnp.int32),
             pltpu.VMEM((half, tile, cols), f32),
             pltpu.VMEM((half, tile, 1), f32),
             pltpu.VMEM(((2 * n - 1) * fetch + 1, tile, cols), f32),
@@ -276,7 +324,7 @@
             pltpu.VMEM((n, hubs, tile, cols), bf16),
             pltpu.VMEM((half, tile, cols), bf16),
             pltpu.VMEM((half, tile, cols), bf16),
-            dma((3,)),
+            dma((5,)),
             dma((nf - 1, CHUNKS)),
             dma((nf - 1, CHUNKS)),
             dma((n - 1,)),
@@ -296,10 +344,10 @@
         ),
         name="sage_layer",
     )(
-        features.reshape(tiles, tile, cols), edge_weights[0], fetch_out, self_cols, neigh_cols,
-        degree.reshape(tiles, tile), bias.reshape(1, cols), idx,
+        features.reshape(tiles, tile, cols), edge_weights[0], fetch_tiles[0], target_slots[0],
+        hub_tiles[0], w_self, w_neigh, degree.reshape(tiles, tile), bias.reshape(1, cols),
     )
-    return result.reshape(half * tile, cols)
+    return jnp.maximum(result.reshape(half * tile, cols), 0)
 
 
 def solution(mesh):

time: 71.8 us -> 65.3 us (0.909)
  the two profiles are of different devices: /device:TPU:25 before, /device:TPU:9 now
where the time goes in v2:
time: 65.3 us; the launch traced here: 65.1 us
  Pallas kernels  61.9 us (95%)
  other arithmetic  1.87 us (3%)
  local copies, waits for them, and re-layouts  1.34 us (2%)
    pallas_call x1, Pallas kernels, body(): pl.pallas_call(functools.partial(kernel, n, nf, fetch, hubs), out_shape=j...  61.9 us
    max x1, other arithmetic, body(): return jnp.maximum(result.reshape(half * tile, cols), 0)  1.87 us

profile of v2, /device:TPU:9, one launch (start us, length us, event | category | flops | bytes accessed | tf_op | source)
XLA Modules:
  0.0 65.1 jit_solution(10993681579398555777)
XLA Ops:
  0.0 0.0 copy-start
  0.0 0.7 %copy-done = s32[1,4,2]{1,2,0:T(2,128)S(1)} copy-done((s32[1,4,2]{1,2,0:T(2,128)S(1)}, s32[1,4,2]{1,2,0:T(2,128)}, u32[]{:S(2)}) %copy-start) | copy-done | bytes 56
  0.7 0.7 %copy.10.hub_tiles = s32[4,2]{1,0:T(4,128)} copy(s32[4,2]{0,1:T(2,128)S(1)} %bitcast.14) | data formatting | bytes 64 | tf_op jit(solution)/shard_map/squeeze | solution.py:348
  1.3 61.9 %sage_layer.1 = bf16[8,128,256]{2,1,0:T(8,128)(2,1)} custom-call(bf16[16,128,256]{2,1,0:T(8,128)(2,1)} %bitcast.8, bf16[4,8,128,128]{3,2,1,0:T(8,128)(2,1)} %bitcast.9, s32[4,8]{1,0:T(4,128)} %bitcast.11, s32[4,8]{1,0:T(4,128)} %bitcast.12, s32[4,2]{1,0:T(4,128)} %copy.10.hub_tiles, bf16[512,512]{1,0:T(8,128)(2,1)} %w_self_in.1, ...), custom_call_target="tpu_custom_call" | custom-call | tf_op jit(solution)/shard_map/sage_layer/pallas_call | solution.py:302
  63.2 1.9 %broadcast_maximum_fusion = bf16[8,128,256]{2,1,0:T(8,128)(2,1)} fusion(bf16[8,128,256]{2,1,0:T(8,128)(2,1)} %sage_layer.1), kind=kLoop, calls=%fused_computation | loop fusion | flops 262144 | bytes 1048576 | tf_op jit(solution)/shard_map/max | solution.py:350
Async XLA Ops:
  0.0 0.7 %copy-start = (s32[1,4,2]{1,2,0:T(2,128)S(1)}, s32[1,4,2]{1,2,0:T(2,128)}, u32[]{:S(2)}) copy-start(s32[1,4,2]{1,2,0:T(2,128)} %param.13) | copy-start | bytes 100

commit v3 on v2

--- a/solution.py
+++ b/solution.py
@@ -17,9 +17,9 @@
 
 def kernel(
     n, nf, fetch, hubs,
-    feats, edges, fetch_tiles, targets, hub_tiles, w_self_in, w_neigh_in, degree, bias, out,
-    xbuf, wts, w_self, w_neigh, fetch_out, fetch_in, fetch_s, prev, last, prev2, last2, own_proj, inv, acc, acc2, hub_out, hub_in, sib_out, sib_in,
-    local_sem, xs, xr, fs, fr, zs, zr, ss, sr, hs, hr, bs, br, *ys,
+    feats, edges, fetch_in_hbm, targets_in, hub_tiles_in, w_self_in, w_neigh_in, degree_in, bias_in,
+    out_hbm, fetch_tiles, targets, hub_tiles, degree, bias, out, xbuf, wts, w_self, w_neigh, fetch_out, fetch_in, fetch_s, prev, last, prev2, last2, own_proj, inv, acc, acc2, hub_out, hub_in, sib_out, sib_in,
+    local_sem, xs, xr, fs, fr, zs, zr, ss, sr, hs, hr, bs, br, out_sem, *ys,
 ):
     me = lax.axis_index("nodes")
     mf = lax.axis_index("feat")
@@ -71,6 +71,12 @@
     def exists(way, k):
         return me >= k if way == 0 else me + k < n
 
+    barrier = pltpu.get_barrier_semaphore()
+    for d in range(1, nf):
+        pl.semaphore_signal(barrier, inc=1, device_id={"feat": lax.rem(mf + d, nf)}, device_id_type=MESH)
+    for d in range(1, n):
+        pl.semaphore_signal(barrier, inc=1, device_id={"nodes": lax.rem(me + d, n)}, device_id_type=MESH)
+    pl.semaphore_signal(barrier, inc=1, device_id={"sub": 1 - u}, device_id_type=MESH)
     own_copy = pltpu.make_async_copy(feats.at[pl.ds(u * half, half)], xbuf.at[0], local_sem.at[0])
     own_copy.start()
     w_copies = []
@@ -82,21 +88,23 @@
     wts_copy = pltpu.make_async_copy(edges, wts, local_sem.at[1])
     wts_copy.start()
 
+    small = []
+    for i, (src, dst) in enumerate((
+        (fetch_in_hbm, fetch_tiles), (targets_in, targets), (hub_tiles_in, hub_tiles),
+        (degree_in, degree), (bias_in, bias),
+    )):
+        small.append(pltpu.make_async_copy(src, dst, local_sem.at[5 + i]))
+        small[-1].start()
+
+    pl.semaphore_wait(barrier, nf + n - 1)
+
+    for c in range(CHUNKS):
+        for d in range(1, nf):
+            x_copy(d, c).start()
+    small[0].wait()
     fetch_out[...] = jnp.zeros_like(fetch_out)
     for t in range(n):
         fetch_out[t, 0:1, 0:fetch] = fetch_tiles[t:t + 1, :]
-
-    barrier = pltpu.get_barrier_semaphore()
-    for d in range(1, nf):
-        pl.semaphore_signal(barrier, inc=1, device_id={"feat": lax.rem(mf + d, nf)}, device_id_type=MESH)
-    for d in range(1, n):
-        pl.semaphore_signal(barrier, inc=1, device_id={"nodes": lax.rem(me + d, n)}, device_id_type=MESH)
-    pl.semaphore_signal(barrier, inc=1, device_id={"sub": 1 - u}, device_id_type=MESH)
-    pl.semaphore_wait(barrier, nf + n - 1)
-
-    for c in range(CHUNKS):
-        for d in range(1, nf):
-            x_copy(d, c).start()
     for d in range(1, n):
         f_copy(d).start()
     fetch_in[0] = fetch_out[me]
@@ -157,6 +165,8 @@
             pl.when(exists(1 - way, 1))(lambda: z_copy(way, 0, c).start())
         s_copy(0, c, u).start()
         if c == 0:
+            small[1].wait()
+            small[2].wait()
             link_hubs()
         elif c <= len(spots):
             way, k = spots[c - 1]
@@ -164,23 +174,26 @@
     for way, k in spots[CHUNKS - 1:]:
         pl.when(exists(way, k))(functools.partial(link, way, k))
 
-    for d in range(1, n):
-        f_copy(d).wait_recv()
-    to_smem = pltpu.make_async_copy(fetch_in, fetch_s, local_sem.at[2])
-    to_smem.start()
-    diagonal = lax.broadcasted_iota(jnp.int32, (tile, tile), 0) == lax.broadcasted_iota(
-        jnp.int32, (tile, tile), 1
-    )
-    w_copies[1].wait()
-    for c in range(CHUNKS):
-        own_proj[c * per:(c + 1) * per] = (project(w_self, c) + bias[...]).reshape(per, tile, cols)
-    for t in range(half):
-        row = 1.0 / degree[pl.ds(u * half + t, 1), :].astype(jnp.float32)
-        inv[t] = jnp.sum(
-            jnp.where(diagonal, jnp.broadcast_to(row, (tile, tile)), 0.0), axis=1, keepdims=True
-        )
-    wts_copy.wait()
-    to_smem.wait()
+    def prepare():
+        for d in range(1, n):
+            f_copy(d).wait_recv()
+        to_smem = pltpu.make_async_copy(fetch_in, fetch_s, local_sem.at[2])
+        to_smem.start()
+        diagonal = lax.broadcasted_iota(jnp.int32, (tile, tile), 0) == lax.broadcasted_iota(
+            jnp.int32, (tile, tile), 1
+        )
+        w_copies[1].wait()
+        small[3].wait()
+        small[4].wait()
+        for c in range(CHUNKS):
+            own_proj[c * per:(c + 1) * per] = (project(w_self, c) + bias[...]).reshape(per, tile, cols)
+        for t in range(half):
+            row = 1.0 / degree[pl.ds(u * half + t, 1), :].astype(jnp.float32)
+            inv[t] = jnp.sum(
+                jnp.where(diagonal, jnp.broadcast_to(row, (tile, tile)), 0.0), axis=1, keepdims=True
+            )
+        wts_copy.wait()
+        to_smem.wait()
 
     def contribute(way, k):
         p = place(way, k)
@@ -204,12 +217,12 @@
         for c in range(CHUNKS):
             for way in range(2):
                 pl.when(exists(way, k))(functools.partial(arrive, way, k, c))
-            if c == 0:
-                if k == 1:
-                    contribute(0, 0)
-                else:
-                    for way in range(2):
-                        pl.when(exists(way, k - 1))(functools.partial(contribute, way, k - 1))
+            if c == 0 and k > 1:
+                for way in range(2):
+                    pl.when(exists(way, k - 1))(functools.partial(contribute, way, k - 1))
+        if k == 1:
+            prepare()
+            contribute(0, 0)
     for way in range(2):
         pl.when(exists(way, n - 1))(functools.partial(contribute, way, n - 1))
 
@@ -249,6 +262,9 @@
                 jnp.float32
             )
 
+    def o_copy(t):
+        return pltpu.make_async_copy(out.at[t], out_hbm.at[t], out_sem.at[t])
+
     def total(t):
         return acc[last[t]] + acc2[last2[t]]
 
@@ -260,6 +276,7 @@
         b_copy(t).wait_recv()
         pre = own_proj[t] + (mine + sib_in[t].astype(jnp.float32)) * inv[t]
         out[t] = pre.astype(jnp.bfloat16)
+        o_copy(t).start()
 
     for c in range(CHUNKS):
         for d in range(1, nf):
@@ -269,6 +286,7 @@
         h_copy(d).wait_send()
     for t in range(half):
         b_copy(t).wait_send()
+        o_copy(t).wait()
 
     for c in range(CHUNKS):
         s_copy(0, c, u).wait_send()
@@ -295,16 +313,20 @@
     depth = w_self.shape[0]
 
     bf16, f32 = jnp.bfloat16, jnp.float32
-    vmem = pl.BlockSpec(memory_space=pltpu.VMEM)
     hbm = pl.BlockSpec(memory_space=pl.ANY)
-    smem = pl.BlockSpec(memory_space=pltpu.SMEM)
     dma = pltpu.SemaphoreType.DMA
     result = pl.pallas_call(
         functools.partial(kernel, n, nf, fetch, hubs),
         out_shape=jax.ShapeDtypeStruct((half, tile, cols), bf16),
-        in_specs=[hbm, hbm, vmem, smem, smem, hbm, hbm, vmem, vmem],
-        out_specs=vmem,
+        in_specs=[hbm] * 9,
+        out_specs=hbm,
         scratch_shapes=[
+            pltpu.VMEM((n, fetch), jnp.int32),
+            pltpu.SMEM((n, fetch), jnp.int32),
+            pltpu.SMEM((n, hubs), jnp.int32),
+            pltpu.VMEM((tiles, tile), jnp.int32),
+            pltpu.VMEM((1, cols), f32),
+            pltpu.VMEM((half, tile, cols), bf16),
             pltpu.VMEM((nf, half, tile, cols), bf16),
             pltpu.VMEM((n, fetch, tile, tile), bf16),
             pltpu.VMEM((depth, cols), bf16),
@@ -324,7 +346,7 @@
             pltpu.VMEM((n, hubs, tile, cols), bf16),
             pltpu.VMEM((half, tile, cols), bf16),
             pltpu.VMEM((half, tile, cols), bf16),
-            dma((5,)),
+            dma((10,)),
             dma((nf - 1, CHUNKS)),
             dma((nf - 1, CHUNKS)),
             dma((n - 1,)),
@@ -335,6 +357,7 @@
             dma((2 * n - 1, CHUNKS)),
             dma((n - 1,)),
             dma((n - 1,)),
+            dma((half,)),
             dma((half,)),
             dma((half,)),
         ]

time: 65.3 us -> 64.3 us (0.985)
  Pallas kernels: 61.9 us -> 60.9 us
    pallas_call x1, Pallas kernels: 61.9 us -> 60.9 us  [body(): pl.pallas_call(functools.partial(kernel, n, nf, fetch, hubs), out_shape=j...]
where the time goes in v3:
time: 64.3 us; the launch traced here: 64.1 us
  Pallas kernels  60.9 us (95%)
  other arithmetic  1.87 us (3%)
  local copies, waits for them, and re-layouts  1.34 us (2%)
    pallas_call x1, Pallas kernels, body(): pl.pallas_call(functools.partial(kernel, n, nf, fetch, hubs), out_shape=j...  60.9 us
    max x1, other arithmetic, body(): return jnp.maximum(result.reshape(half * tile, cols), 0)  1.87 us

profile of v3, /device:TPU:9, one launch (start us, length us, event | category | flops | bytes accessed | tf_op | source)
XLA Modules:
  0.0 64.1 jit_solution(2786283584050016041)
XLA Ops:
  0.0 0.0 copy-start
  0.0 0.7 %copy-done = s32[1,4,2]{1,2,0:T(2,128)S(1)} copy-done((s32[1,4,2]{1,2,0:T(2,128)S(1)}, s32[1,4,2]{1,2,0:T(2,128)}, u32[]{:S(2)}) %copy-start) | copy-done | bytes 56
  0.7 0.7 %copy.10.hub_tiles_in = s32[4,2]{1,0:T(4,128)} copy(s32[4,2]{0,1:T(2,128)S(1)} %bitcast.14) | data formatting | bytes 64 | tf_op jit(solution)/shard_map/squeeze | solution.py:371
  1.3 60.9 %sage_layer.1 = bf16[8,128,256]{2,1,0:T(8,128)(2,1)} custom-call(bf16[16,128,256]{2,1,0:T(8,128)(2,1)} %bitcast.8, bf16[4,8,128,128]{3,2,1,0:T(8,128)(2,1)} %bitcast.9, s32[4,8]{1,0:T(4,128)} %bitcast.11, s32[4,8]{1,0:T(4,128)} %bitcast.12, s32[4,2]{1,0:T(4,128)} %copy.10.hub_tiles_in, bf16[512,512]{1,0:T(8,128)(2,1)} %w_self_in.1, ...), custom_call_target="tpu_custom_call" | custom-call | tf_op jit(solution)/shard_map/sage_layer/pallas_call | solution.py:318
  62.2 1.9 %broadcast_maximum_fusion = bf16[8,128,256]{2,1,0:T(8,128)(2,1)} fusion(bf16[8,128,256]{2,1,0:T(8,128)(2,1)} %sage_layer.1), kind=kLoop, calls=%fused_computation | loop fusion | flops 262144 | bytes 1048576 | tf_op jit(solution)/shard_map/max | solution.py:373
Async XLA Ops:
  0.0 0.7 %copy-start = (s32[1,4,2]{1,2,0:T(2,128)S(1)}, s32[1,4,2]{1,2,0:T(2,128)}, u32[]{:S(2)}) copy-start(s32[1,4,2]{1,2,0:T(2,128)} %param.13) | copy-start | bytes 100
